TPU v7x, 32 devices: a whole 2x2x4 slice. The times are simulated.
32 devices in a mesh: wide: 16 (over z, x, core), narrow: 2 (over y).
Axes of the slice: x: 2, y: 2, z: 4, core: 2. Of those that a mesh axis runs over, the one named last changes fastest.
Arguments:
- fields: bfloat16 [2, 512, 64, 1024], P(None, 'wide', 'narrow'), may hold values from -6 to 6
- vel_x: float32 [512], P('wide'), may hold values from -1 to 1
- vel_y: float32 [512], P('wide'), may hold values from -1 to 1
- collision: bfloat16 [1024, 1024], replicated, may hold values from -1 to 2
Outputs:
- smoothed: bfloat16 [2, 512, 64, 1024], P(None, 'wide', 'narrow')
All inputs are finite; a program needn't handle non-finite values.
Results may differ from a plain program's by a relative error of at most 0.001.
The roundings to bfloat16 on the way count: a program that leaves them out, or rounds other values in their place, can miss the bound.
Values may be sent and summed in bfloat16 or wider, within the bound.
A program may use at most 192 MiB of HBM per device.

v0:
```python
import jax
import jax.numpy as jnp
import numpy as np
from jax import lax
from jax.sharding import PartitionSpec as P

time_step = 0.02
lift_gain = 24.0
upwind_share = 0.5


def from_behind(block, axis, distance):
    devices = range(lax.axis_size(axis))
    route = [((i - distance) % len(devices), i) for i in devices]
    return lax.ppermute(block, axis, route)


def volume_table():
    points_ref = -np.cos(np.pi * np.arange(8) / 7.0)
    identity = np.eye(8)
    differ = points_ref[:, None] - points_ref[None, :] + identity
    weights = 1.0 / np.prod(differ, axis=1)
    derivative = weights[None, :] / weights[:, None] / differ * (1.0 - identity)
    derivative = derivative - identity * derivative.sum(axis=1)[:, None]
    along_x = np.kron(np.eye(2), np.kron(derivative, np.eye(8)))
    along_y = np.kron(np.eye(2), np.kron(np.eye(8), derivative))
    joined = np.concatenate([along_x.T, along_y.T], axis=1)
    return jnp.asarray(joined, dtype=jnp.float32).astype(jnp.bfloat16)


def sweep(current, speed_x, speed_y, from_prev, from_next, table):
    shape = current.shape
    lanes = shape[3]
    pairs = current.reshape(shape[0], shape[1], shape[2], lanes // 128, 128)
    slopes = jnp.dot(pairs, table, preferred_element_type=jnp.float32)
    grad_x = slopes[..., :128].reshape(shape)
    grad_y = slopes[..., 128:].reshape(shape)
    values = current.astype(jnp.float32)
    index = lax.iota(jnp.int32, lanes)
    node_p = index // 8 % 8
    node_q = index % 8
    first_p = (node_p == 0).astype(jnp.float32)
    last_p = (node_p == 7).astype(jnp.float32)
    first_q = (node_q == 0).astype(jnp.float32)
    last_q = (node_q == 7).astype(jnp.float32)
    below = jnp.roll(values, 57, axis=3)
    above = jnp.roll(values, -57, axis=3)
    coef_x = speed_x[:, :, None, None]
    coef_y = speed_y[:, :, None, None]
    plus_x = 0.5 * (coef_x + upwind_share * jnp.abs(coef_x))
    minus_x = 0.5 * (coef_x - upwind_share * jnp.abs(coef_x))
    plus_y = 0.5 * (coef_y + upwind_share * jnp.abs(coef_y))
    minus_y = 0.5 * (coef_y - upwind_share * jnp.abs(coef_y))
    change_x = -coef_x * grad_x + lift_gain * (
        minus_x * last_p * (values - from_next) + plus_x * first_p * (from_prev - values)
    )
    change_y = -coef_y * grad_y + lift_gain * (
        minus_y * last_q * (values - above) + plus_y * first_q * (below - values)
    )
    return (values + time_step * (change_x + change_y)).astype(jnp.bfloat16)


def collide_block(block, collision):
    shape = block.shape
    flat = block.reshape(shape[0] * shape[1], -1)
    mixed = jnp.dot(collision, flat, preferred_element_type=jnp.float32)
    return mixed.astype(jnp.bfloat16).reshape(shape)


def shards(fields, vel_x, vel_y, collision):
    table = volume_table()
    signs = jnp.array([1.0, -1.0], jnp.float32)
    shape = fields.shape
    lanes = shape[3]
    erows = lanes // 64
    values = fields.astype(jnp.float32)
    last_column = fields[:, :, shape[2] - 1, :].reshape(shape[0], shape[1], erows, 8, 8)
    first_column = fields[:, :, 0, :].reshape(shape[0], shape[1], erows, 8, 8)
    right_trace = last_column[:, :, :, 7, :].reshape(shape[0], shape[1], erows * 8)
    left_trace = first_column[:, :, :, 0, :].reshape(shape[0], shape[1], erows * 8)
    from_left = from_behind(right_trace, "narrow", 1)
    from_right = from_behind(left_trace, "narrow", -1)
    edge_prev = jnp.pad(
        from_left.reshape(shape[0], shape[1], erows, 1, 8), ((0, 0), (0, 0), (0, 0), (0, 7), (0, 0))
    )
    edge_prev = edge_prev.reshape(shape[0], shape[1], 1, lanes).astype(jnp.float32)
    edge_next = jnp.pad(
        from_right.reshape(shape[0], shape[1], erows, 1, 8),
        ((0, 0), (0, 0), (0, 0), (7, 0), (0, 0)),
    )
    edge_next = edge_next.reshape(shape[0], shape[1], 1, lanes).astype(jnp.float32)
    from_prev = jnp.concatenate([edge_prev, jnp.roll(values, -56, axis=3)[:, :, :-1]], axis=2)
    from_next = jnp.concatenate([jnp.roll(values, 56, axis=3)[:, :, 1:], edge_next], axis=2)
    moved = sweep(
        fields,
        signs[:, None] * vel_x[None, :],
        signs[:, None] * vel_y[None, :],
        from_prev,
        from_next,
        table,
    )
    return lax.all_to_all(
        collide_block(
            lax.all_to_all(moved, "wide", split_axis=2, concat_axis=1, tiled=True), collision
        ),
        "wide",
        split_axis=1,
        concat_axis=2,
        tiled=True,
    )


def solution(mesh):
    return jax.shard_map(
        shards,
        mesh=mesh,
        in_specs=(P(None, "wide", "narrow", None), P("wide"), P("wide"), P()),
        out_specs=P(None, "wide", "narrow", None),
        check_vma=False,
    )
```

profile of v0, /device:TPU:1, one launch (start us, length us, event | category | flops | bytes accessed | tf_op | source)
XLA Modules:
  0.0 327.8 jit_solution(4259069553683424123)
XLA Ops:
  0.0 0.0 copy-start
  0.0 2.1 fusion.37
  2.2 0.3 copy.49
  2.5 2.1 collective-permute-start
  4.6 1.0 copy.50
  5.6 0.0 copy-start.1
  5.6 1.0 slice_bitcast_fusion.2
  6.6 0.0 collective-permute-start.1
  6.7 3.1 fusion.35
  9.8 2.8 fusion.39
  12.7 0.0 copy-done.1
  12.7 8.0 %fusion.38 = (f32[2,32,32,967]{3,2,1,0:T(8,128)}, f32[2,32,32,967]{3,2,1,0:T(8,128)}) fusion(bf16[2,32,32,1024]{3,2,1,0:T(8,128)(2,1)S(1)} %copy-done.1), kind=kLoop, calls=%fused_computation.76 | loop fusion | bytes 31686656 | tf_op jit(solution)/shard_map/jit(_roll_static)/slice | solution.py:47
  20.7 0.0 copy-start.3
  20.7 8.2 %fusion.36 = (f32[2,32,32,968]{3,2,1,0:T(8,128)}, f32[2,32,32,968]{3,2,1,0:T(8,128)}) fusion(bf16[2,32,32,1024]{3,2,1,0:T(8,128)(2,1)S(1)} %copy-done.1), kind=kLoop, calls=%fused_computation.74 | loop fusion | bytes 31719424 | tf_op jit(solution)/shard_map/jit(_roll_static)/slice | solution.py:93
  28.8 0.0 copy-done.3
  28.8 8.1 %convolution_bitcast_fusion = f32[2,32,32,8,256]{4,2,3,1,0:T(8,128)} fusion(bf16[128,256,1,1,1]{1,0,4,3,2:T(8,128)(2,1)S(1)} %copy-done.3, bf16[2,32,32,1024]{3,2,1,0:T(8,128)(2,1)S(1)} %copy-done.1), kind=kOutput, calls=%fused_computation.26 | convolution fusion | flops 1073741824 | bytes 21037056 | tf_op jit(solution)/shard_map/dot_general | solution.py:35
  36.9 0.0 copy-start.4
  36.9 0.0 copy-start.5
  36.9 0.0 copy-start.6
  36.9 11.2 %slice_bitcast_fusion.1 = (f32[2,32,8,4,8,128]{5,4,3,2,1,0:T(8,128)}, f32[2,32,8,4,8,128]{5,4,3,2,1,0:T(8,128)}) fusion(f32[2,32,32,8,256]{4,2,3,1,0:T(8,128)} %convolution_bitcast_fusion), kind=kLoop, calls=%fused_computation.24 | loop fusion | bytes 33554432
  48.1 0.0 copy-done.4
  48.1 0.0 copy-done.5
  48.1 0.0 copy-done.6
  48.1 0.0 copy-start.2
  48.1 0.1 multiply_negate_fusion.1
  48.2 0.9 broadcast_multiply_fusion.2
  49.1 0.9 broadcast_multiply_fusion
  50.0 0.0 collective-permute-done.1
  50.0 0.1 pad_convert_fusion
  50.1 1.1 copy.39
  51.2 1.5 copy.40
  52.8 0.0 collective-permute-done
  52.8 0.1 pad_convert_fusion.1
  52.9 1.1 copy.36
  54.0 2.2 copy.37
  56.2 0.0 copy-done.2
  56.2 22.0 %fusion.14 = bf16[2,32,32,1024]{3,2,1,0:T(8,128)(2,1)S(1)} fusion(f32[2,32,32,967]{3,2,1,0:T(8,128)} %get-tuple-element.14, f32[2,32,32,57]{3,2,1,0:T(8,128)} %get-tuple-element.16, f32[2,32,32,57]{3,2,1,0:T(8,128)} %get-tuple-element.15, f32[2,32,32,967]{3,2,1,0:T(8,128)} %get-tuple-element.13, f32[2,32,8,4,8,128]{5,4,3,2,1,0:T(8,128)} %get-tuple-element.6, ...), kind=kLoop, calls=%fused_computation.25 | loop fusion | flops 56623104 | bytes 60293632 | tf_op jit(solution)/shard_map/convert_element_type | solution.py:60
  78.3 2.3 copy.42
  80.6 99.4 %all_to_all.33 = bf16[2,32,32,1024]{3,1,0,2:T(8,128)(2,1)S(1)} all-to-all(bf16[2,32,32,1024]{3,1,0,2:T(8,128)(2,1)S(1)} %copy.42), channel_id=1, replica_groups=mesh['wide'=16,'narrow'=2] {'wide'}, dimensions={2} | all-to-all | bytes 8388608 | tf_op jit(solution)/shard_map/all_to_all | solution.py:104
  180.0 6.3 %copy.43 = bf16[2,32,16,2,1024]{4,3,1,2,0:T(2,128)(2,1)} copy(bf16[2,32,16,2,1024]{4,1,0,3,2:T(8,128)(2,1)S(1)} %bitcast.54) | data formatting | bytes 8388608 | tf_op jit(solution)/shard_map/all_to_all | solution.py:104
  186.4 3.6 %copy.54 = bf16[128,8,2,1024]{3,1,2,0:T(8,128)(2,1)S(1)} copy(bf16[128,8,2,1024]{3,2,1,0:T(2,128)(2,1)} %bitcast.55) | data formatting | bytes 8388608
  190.0 0.0 copy-done
  190.0 6.3 %convert_bitcast_fusion = bf16[1024,2048]{0,1:T(8,128)(2,1)} fusion(bf16[1024,2048]{1,0:T(8,128)(2,1)S(1)} %bitcast.60, bf16[1024,1024]{1,0:T(8,128)(2,1)S(1)} %copy-done), kind=kOutput, calls=%fused_computation.29 | convolution fusion | flops 4297064448 | bytes 10485760 | tf_op jit(solution)/shard_map/dot_general | solution.py:66
  196.3 7.8 %reshape.295 = bf16[2,512,2,1024]{1,0,3,2:T(2,128)(2,1)} reshape(bf16[1024,2048]{0,1:T(8,128)(2,1)} %convert_bitcast_fusion) | data formatting | bytes 8388608 | tf_op jit(solution)/shard_map/reshape | solution.py:67
  204.1 19.7 %copy.44 = bf16[2,512,2,1024]{3,2,0,1:T(2,128)(2,1)} copy(bf16[2,512,2,1024]{1,0,3,2:T(2,128)(2,1)} %reshape.295) | data formatting | bytes 8388608 | tf_op jit(solution)/shard_map/reshape | solution.py:67
  223.8 97.6 %all_to_all.34 = bf16[2,512,2,1024]{3,2,0,1:T(2,128)(2,1)S(1)} all-to-all(bf16[2,512,2,1024]{3,2,0,1:T(2,128)(2,1)} %copy.44), channel_id=1, replica_groups=mesh['wide'=16,'narrow'=2] {'wide'}, dimensions={1} | all-to-all | bytes 8388608 | tf_op jit(solution)/shard_map/all_to_all | solution.py:102
  321.3 1.4 copy.45
  322.7 0.8 copy.46
  323.5 4.3 %copy.47 = bf16[2,32,32,1024]{3,2,1,0:T(8,128)(2,1)} copy(bf16[2,32,32,1024]{3,1,2,0:T(8,128)(2,1)S(1)} %bitcast.57) | data formatting | bytes 8388608 | tf_op jit(solution)/shard_map/all_to_all | solution.py:102
  (5 shorter events, 0.0 us)
Async XLA Ops:
  0.0 190.0 %copy-start = (bf16[1024,1024]{1,0:T(8,128)(2,1)S(1)}, bf16[1024,1024]{1,0:T(8,128)(2,1)}, u32[]{:S(2)}) copy-start(bf16[1024,1024]{1,0:T(8,128)(2,1)} %param.9) | copy-start | bytes 6291460
  2.5 50.3 %collective-permute-start = (bf16[2,32,128]{1,2,0:T(8,128)(2,1)S(1)}, bf16[2,32,128]{1,2,0:T(8,128)(2,1)S(1)}, u32[]{:S(2)}, u32[]{:S(2)}) collective-permute-start(bf16[2,32,128]{1,2,0:T(8,128)(2,1)S(1)} %slice_bitcast_fusion.3), channel_id=1, source_target_pairs={{1,0},{0,1},{3,2},{2,3},{5,4},{4,5},{7,6},{6,7},{9,8},{8,9},{11,10... | collective-permute-start | bytes 49160 | tf_op jit(solution)/shard_map/ppermute | solution.py:15
  5.6 7.0 %copy-start.1 = (bf16[2,32,32,1024]{3,2,1,0:T(8,128)(2,1)S(1)}, bf16[2,32,32,1024]{3,2,1,0:T(8,128)(2,1)}, u32[]{:S(2)}) copy-start(bf16[2,32,32,1024]{3,2,1,0:T(8,128)(2,1)} %param.6) | copy-start | bytes 12582916
  6.6 43.4 %collective-permute-start.1 = (bf16[2,32,128]{1,2,0:T(8,128)(2,1)S(1)}, bf16[2,32,128]{1,2,0:T(8,128)(2,1)S(1)}, u32[]{:S(2)}, u32[]{:S(2)}) collective-permute-start(bf16[2,32,128]{1,2,0:T(8,128)(2,1)S(1)} %slice_bitcast_fusion.2), channel_id=1, source_target_pairs={{1,0},{0,1},{3,2},{2,3},{5,4},{4,5},{7,6},{6,7},{9,8},{8,9},{11,10... | collective-permute-start | bytes 49160 | tf_op jit(solution)/shard_map/ppermute | solution.py:15
  20.7 8.2 %copy-start.3 = (bf16[128,256,1,1,1]{1,0,4,3,2:T(8,128)(2,1)S(1)}, bf16[128,256,1,1,1]{1,0,4,3,2:T(8,128)(2,1)}, u32[]{:S(2)}) copy-start(bf16[128,256,1,1,1]{1,0,4,3,2:T(8,128)(2,1)} %constant.60) | copy-start | bytes 196612
  36.9 11.2 %copy-start.4 = (f32[32]{0:T(128)S(1)}, f32[32]{0:T(128)}, u32[]{:S(2)}) copy-start(f32[32]{0:T(128)} %param.7) | copy-start | bytes 388
  36.9 11.2 %copy-start.5 = (f32[32]{0:T(128)S(1)}, f32[32]{0:T(128)}, u32[]{:S(2)}) copy-start(f32[32]{0:T(128)} %param.8) | copy-start | bytes 388
  36.9 11.2 %copy-start.6 = (f32[2]{0:T(128)S(1)}, f32[2]{0:T(128)}, u32[]{:S(2)}) copy-start(f32[2]{0:T(128)} %constant.54.clone) | copy-start | bytes 28
  48.1 8.2 %copy-start.2 = (f32[2,32,32,56]{3,2,1,0:T(8,128)S(1)}, f32[2,32,32,56]{3,2,1,0:T(8,128)}, u32[]{:S(2)}) copy-start(f32[2,32,32,56]{3,2,1,0:T(8,128)} %get-tuple-element.7) | copy-start | bytes 1376260
where the time goes:
time: 329 us; the launch traced here: 328 us
  blocking collectives  197 us (60%)
  local copies, waits for them, and re-layouts  90.1 us (27%)
  other arithmetic  24.1 us (7%)
  matrix products  14.4 us (4%)
    all_to_all x1, blocking collectives, shards(): lax.all_to_all(moved, 'wide', split_axis=2, concat_axis=1, tiled=True)  99.4 us
    all_to_all x1, blocking collectives, shards(): lax.all_to_all(collide_block(lax.all_to_all(moved, 'wide', split_axis=2,...  97.6 us
    reshape x2, local copies, waits for them, and re-layouts, collide_block(): return mixed.astype(jnp.bfloat16).reshape(shape)  27.5 us
    convert_element_type x1, other arithmetic, sweep(): return (values + time_step * (change_x + change_y)).astype(jnp.bfloat16)  22 us
    unnamed x18, local copies, waits for them, and re-layouts  16.1 us
    slice x2, local copies, waits for them, and re-layouts, shards(): jnp.roll(values, 56, axis=3)[:, :, 1:]  11.3 us
    slice x2, local copies, waits for them, and re-layouts, sweep(): above = jnp.roll(values, -57, axis=3)  10.8 us
    dot_general x1, matrix products, sweep(): slopes = jnp.dot(pairs, table, preferred_element_type=jnp.float32)  8.06 us
  transfers between devices with their start and end apart: 2, of which 0 were waited for; matrix products, arithmetic and copies ran while one was open for 15% of the time, Pallas kernels for 0%

commit v1 on v0

v1 whole, which is shorter than its diff:
```python
import functools

import jax
import jax.numpy as jnp
import numpy as np
from jax import lax
from jax.experimental import pallas as pl
from jax.experimental.pallas import tpu as pltpu
from jax.sharding import PartitionSpec as P

time_step = 0.02
lift_gain = 24.0
upwind_share = 0.5
GROUP = 16
CHUNK = 128
TILE = 256
MESH = pl.DeviceIdType.MESH


def derivative_matrix():
    points_ref = -np.cos(np.pi * np.arange(8) / 7.0)
    identity = np.eye(8)
    differ = points_ref[:, None] - points_ref[None, :] + identity
    weights = 1.0 / np.prod(differ, axis=1)
    derivative = weights[None, :] / weights[:, None] / differ * (1.0 - identity)
    return derivative - identity * derivative.sum(axis=1)[:, None]


def as_table(matrix):
    return jnp.asarray(matrix, dtype=jnp.float32).astype(jnp.bfloat16)


def lane_tables():
    derivative = derivative_matrix()
    along_x = np.kron(np.eye(2), np.kron(derivative, np.eye(8)))
    along_y = np.kron(np.eye(2), np.kron(np.eye(8), derivative))
    slopes = np.concatenate([along_x.T, along_y.T], axis=1)
    lane = np.arange(CHUNK)
    p, q = lane // 8 % 8, lane % 8
    faces_x = np.zeros((2 * CHUNK, CHUNK))
    first, last = lane[p == 0], lane[p == 7]
    faces_x[first + 56, first] = 1.0
    faces_x[CHUNK + last - 56, last] = 1.0
    faces_y = np.zeros((3 * CHUNK, CHUNK))
    for target in lane[q == 0]:
        source = target - 57
        faces_y[source if source >= 0 else 2 * CHUNK + source, target] = 1.0
    for target in lane[q == 7]:
        source = target + 57
        faces_y[source if source < CHUNK else CHUNK + source, target] = 1.0
    return as_table(slopes), as_table(faces_x), as_table(faces_y)


def swap_table():
    row = np.arange(GROUP * GROUP)
    table = np.zeros((GROUP * GROUP, GROUP * GROUP))
    table[row, row % GROUP * GROUP + row // GROUP] = 1.0
    return as_table(table)


def restore_table(each):
    owners = GROUP // each
    v, column = np.meshgrid(np.arange(GROUP), np.arange(GROUP), indexing="ij")
    source = (column % each * owners + column // each) * GROUP + v
    table = np.zeros((GROUP * GROUP, GROUP * GROUP))
    table[(v * GROUP + column).ravel(), source.ravel()] = 1.0
    return as_table(table)


def sweep_kernel(
    n, strips, each,
    fields, vel_x, vel_y, collision, slopes, faces_x, faces_y, swap,
    result,
    columns, packed, gathered, mixed, coefs,
    edge_send, edge_recv, out_send, out_recv, back_send, back_recv, own_sem,
):
    me = lax.axis_index("wide")
    strip = lax.axis_index("narrow")
    pairs, local, width, lanes = fields.shape
    rows = pairs * local
    speeds = n * local
    chunks = lanes // CHUNK
    above, below = lax.rem(strip + 1, strips), lax.rem(strip + strips - 1, strips)

    barrier = pltpu.get_barrier_semaphore()

    def greet(i, carry):
        pl.semaphore_signal(
            barrier, inc=1, device_id={"wide": lax.rem(me + i, n)}, device_id_type=MESH
        )
        return carry

    lax.fori_loop(1, n, greet, 0)
    for neighbour in (above, below):
        pl.semaphore_signal(barrier, inc=1, device_id={"narrow": neighbour}, device_id_type=MESH)

    for s in range(pairs):
        for g in range(local // GROUP):
            def turn(h, carry):
                at = pl.multiple_of(h * GROUP, GROUP)
                for t in range(lanes // TILE):
                    part = pl.ds(t * TILE, TILE)
                    block = fields[s, pl.ds(g * GROUP, GROUP), pl.ds(at, GROUP), part]
                    turned = jnp.dot(
                        swap[...], block.reshape(GROUP * GROUP, TILE),
                        preferred_element_type=jnp.float32,
                    )
                    columns[
                        pl.ds(at + 1, GROUP), pl.ds(s * local + g * GROUP, GROUP), part
                    ] = turned.astype(jnp.bfloat16).reshape(GROUP, GROUP, TILE)
                return carry

            lax.fori_loop(0, width // GROUP, turn, 0)

    lane = lax.broadcasted_iota(jnp.int32, (rows, CHUNK), 1)
    node_p = (lane >> 3) & 7
    node_q = lane & 7
    eye = lax.broadcasted_iota(jnp.int32, (local, local), 0) == lax.broadcasted_iota(
        jnp.int32, (local, local), 1
    )

    def signed(vel):
        spread = jnp.broadcast_to(vel[...], (local, local))
        column = jnp.sum(jnp.where(eye, spread, 0.0), axis=1, keepdims=True)
        return jnp.broadcast_to(jnp.concatenate([column, -column], axis=0), (rows, CHUNK))

    lift = time_step * lift_gain
    own = jnp.ones((rows, CHUNK), jnp.float32)
    for k, (speed, node) in enumerate(((signed(vel_x), node_p), (signed(vel_y), node_q))):
        plus = 0.5 * (speed + upwind_share * jnp.abs(speed))
        minus = 0.5 * (speed - upwind_share * jnp.abs(speed))
        face = lift * (jnp.where(node == 0, plus, 0.0) - jnp.where(node == 7, minus, 0.0))
        own = own - face
        coefs[1 + k] = -time_step * speed
        coefs[3 + k] = face
    coefs[0] = own

    pl.semaphore_wait(barrier, n + 1)

    def edge(k):
        source, target, device = ((width, 0, above), (1, width + 1, below))[k]
        return pltpu.make_async_remote_copy(
            src_ref=columns.at[source], dst_ref=columns.at[target],
            send_sem=edge_send.at[k], recv_sem=edge_recv.at[k],
            device_id={"narrow": device}, device_id_type=MESH,
        )

    edge(0).start()
    edge(1).start()

    def outward(c, d, at):
        return pltpu.make_async_remote_copy(
            src_ref=packed.at[c, d],
            dst_ref=gathered.at[c, :, pl.ds(pl.multiple_of(at * local, GROUP), local), :],
            send_sem=out_send.at[c, d], recv_sem=out_recv.at[c, at],
            device_id={"wide": d}, device_id_type=MESH,
        )

    def stacked(value, shift):
        return jnp.concatenate(
            [
                value[:, (m + shift) % chunks * CHUNK : ((m + shift) % chunks + 1) * CHUNK]
                for m in range(chunks)
            ],
            axis=0,
        )

    for c in range(each):
        def transport(i, carry):
            d = lax.rem(me + i, n)
            if c == 0:
                @pl.when(d == 0)
                def _():
                    edge(0).wait_recv()
            if c == each - 1:
                @pl.when(d == n - 1)
                def _():
                    edge(1).wait_recv()
            j = d * each + c
            now = columns[j + 1]
            here = stacked(now, 0)
            slope = jnp.dot(here, slopes[...], preferred_element_type=jnp.float32)
            next_x = jnp.dot(
                jnp.concatenate([stacked(columns[j], 0), stacked(columns[j + 2], 0)], axis=1),
                faces_x[...], preferred_element_type=jnp.float32,
            )
            next_y = jnp.dot(
                jnp.concatenate([here, stacked(now, -1), stacked(now, 1)], axis=1),
                faces_y[...], preferred_element_type=jnp.float32,
            )
            for m in range(chunks):
                span = slice(m * rows, (m + 1) * rows)
                moved = (
                    coefs[0] * here[span].astype(jnp.float32)
                    + coefs[1] * slope[span, :CHUNK]
                    + coefs[2] * slope[span, CHUNK:]
                    + coefs[3] * next_x[span]
                    + coefs[4] * next_y[span]
                )
                packed[c, d, :, :, pl.ds(m * CHUNK, CHUNK)] = moved.astype(jnp.bfloat16).reshape(
                    pairs, local, CHUNK
                )

            @pl.when(i < n)
            def _():
                outward(c, d, me).start()

            return carry

        lax.fori_loop(1, n + 1, transport, 0)
        pltpu.make_async_copy(
            packed.at[c, me],
            gathered.at[c, :, pl.ds(pl.multiple_of(me * local, GROUP), local), :],
            own_sem.at[c],
        ).start()

    def back(c, d, at):
        return pltpu.make_async_remote_copy(
            src_ref=mixed.at[c, d], dst_ref=result.at[c, at],
            send_sem=back_send.at[c, d], recv_sem=back_recv.at[c, at],
            device_id={"wide": d}, device_id_type=MESH,
        )

    for c in range(each):
        pltpu.make_async_copy(
            packed.at[c, me],
            gathered.at[c, :, pl.ds(pl.multiple_of(me * local, GROUP), local), :],
            own_sem.at[c],
        ).wait()

        def arrive(i, carry):
            d = lax.rem(me + n - i, n)
            outward(c, d, d).wait_recv()
            return carry

        lax.fori_loop(1, n, arrive, 0)

        def collide(i, carry):
            d = lax.rem(me + i, n)
            left = jnp.concatenate(
                [
                    collision[pl.ds(pl.multiple_of(s * speeds + d * local, GROUP), local), :]
                    for s in range(pairs)
                ],
                axis=0,
            )
            for t in range(lanes // TILE):
                part = pl.ds(t * TILE, TILE)
                total = jnp.dot(
                    left, gathered[c, :, :, part].reshape(pairs * speeds, TILE),
                    preferred_element_type=jnp.float32,
                )
                mixed[c, d, :, :, part] = total.astype(jnp.bfloat16).reshape(pairs, local, TILE)

            @pl.when(i < n)
            def _():
                back(c, d, me).start()

            return carry

        lax.fori_loop(1, n + 1, collide, 0)
        pltpu.make_async_copy(
            mixed.at[c, me], result.at[c, me], own_sem.at[each + c]
        ).start()

    edge(0).wait_send()
    edge(1).wait_send()
    for c in range(each):
        pltpu.make_async_copy(
            mixed.at[c, me], result.at[c, me], own_sem.at[each + c]
        ).wait()

        def finish(i, carry):
            d = lax.rem(me + i, n)
            outward(c, d, me).wait_send()
            back(c, d, me).wait_send()
            back(c, d, d).wait_recv()
            return carry

        lax.fori_loop(1, n, finish, 0)


def restore_kernel(restore, block, out):
    rows = GROUP * GROUP
    lanes = out.shape[-1]
    turned = jnp.dot(
        restore[...], block[...].reshape(rows, lanes), preferred_element_type=jnp.float32
    )
    out[...] = turned.astype(jnp.bfloat16).reshape(out.shape)


def shards(fields, vel_x, vel_y, collision):
    n = lax.axis_size("wide")
    strips = lax.axis_size("narrow")
    pairs, local, width, lanes = fields.shape
    each = width // n
    rows = pairs * local
    bf16 = jnp.bfloat16
    vmem = pl.BlockSpec(memory_space=pltpu.VMEM)
    dma = pltpu.SemaphoreType.DMA
    returned = pl.pallas_call(
        functools.partial(sweep_kernel, n, strips, each),
        out_shape=jax.ShapeDtypeStruct((each, n, pairs, local, lanes), bf16),
        in_specs=[vmem] * 8,
        out_specs=pl.BlockSpec(memory_space=pl.ANY),
        scratch_shapes=[
            pltpu.VMEM((width + 2, rows, lanes), bf16),
            pltpu.VMEM((each, n, pairs, local, lanes), bf16),
            pltpu.VMEM((each, pairs, n * local, lanes), bf16),
            pltpu.VMEM((each, n, pairs, local, lanes), bf16),
            pltpu.VMEM((5, rows, CHUNK), jnp.float32),
            dma((2,)),
            dma((2,)),
            dma((each, n)),
            dma((each, n)),
            dma((each, n)),
            dma((each, n)),
            dma((2 * each,)),
        ],
        compiler_params=pltpu.CompilerParams(
            collective_id=0, has_side_effects=True, vmem_limit_bytes=48 * 1024 * 1024
        ),
    )(
        fields, vel_x.reshape(1, local), vel_y.reshape(1, local), collision,
        *lane_tables(), swap_table(),
    )
    owners = GROUP // each
    return pl.pallas_call(
        restore_kernel,
        grid=(pairs, local // GROUP, width // GROUP),
        out_shape=jax.ShapeDtypeStruct(fields.shape, bf16),
        in_specs=[
            pl.BlockSpec((GROUP * GROUP, GROUP * GROUP), lambda s, g, h: (0, 0)),
            pl.BlockSpec((each, owners, 1, GROUP, lanes), lambda s, g, h: (0, h, s, g, 0)),
        ],
        out_specs=pl.BlockSpec((1, GROUP, GROUP, lanes), lambda s, g, h: (s, g, h, 0)),
        compiler_params=pltpu.CompilerParams(vmem_limit_bytes=16 * 1024 * 1024),
    )(restore_table(each), returned)


def solution(mesh):
    return jax.shard_map(
        shards,
        mesh=mesh,
        in_specs=(P(None, "wide", "narrow", None), P("wide"), P("wide"), P()),
        out_specs=P(None, "wide", "narrow", None),
        check_vma=False,
    )
```

time: 329 us -> 209 us (0.64)
  the two profiles are of different devices: /device:TPU:1 before, /device:TPU:11 now
where the time goes in v1:
time: 209 us; the launch traced here: 208 us
  Pallas kernels  200 us (96%)
  local copies, waits for them, and re-layouts  8.56 us (4%)
    pallas_call x1, Pallas kernels, shards(): pl.pallas_call(functools.partial(sweep_kernel, n, strips, each), out_shap...  195 us
    unnamed x18, local copies, waits for them, and re-layouts  8.56 us
    pallas_call x1, Pallas kernels, shards(): pl.pallas_call(restore_kernel, grid=(pairs, local // GROUP, width // GROU...  4.95 us

profile of v1, /device:TPU:11, one launch (start us, length us, event | category | flops | bytes accessed | tf_op | source)
XLA Modules:
  0.0 208.2 jit_solution(3785971739368136511)
XLA Ops:
  0.0 0.0 copy-start.1
  0.0 1.6 copy-done.1
  1.6 0.0 copy-start.2
  1.6 0.9 copy-done.2
  2.5 0.0 copy-start.4
  2.5 0.9 copy-done.4
  3.4 0.0 copy-start.5
  3.4 0.8 copy-done.5
  4.2 0.0 copy-start.6
  4.2 0.8 copy-done.6
  5.1 0.0 copy-start.7
  5.1 0.7 copy-done.7
  5.7 0.0 copy-start.8
  5.7 0.7 copy-done.8
  6.4 0.0 copy-start.3
  6.4 194.6 %shard_map.91.block = bf16[2,16,2,32,1024]{4,3,2,1,0:T(8,128)(2,1)} custom-call(bf16[2,32,32,1024]{3,2,1,0:T(8,128)(2,1)} %fields.1, f32[1,32]{1,0:T(1,128)S(1)} %bitcast.2, f32[1,32]{1,0:T(1,128)S(1)} %bitcast.3, bf16[1024,1024]{1,0:T(8,128)(2,1)S(1)} %copy-done.1, bf16[128,256]{1,0:T(8,128)(2,1)S(1)} %copy-done.6, bf16[256,128]{1,0:T(8,128)(2,1)S(1)} %copy-done.5, ...), custom_call_target="tpu_custom_call" | custom-call | tf_op jit(solution)/shard_map/pallas_call | solution.py:301
  201.0 0.0 copy-done.3
  201.0 0.0 copy-start
  201.0 2.2 %copy-done = bf16[2,16,2,32,1024]{4,3,2,1,0:T(8,128)(2,1)S(1)} copy-done((bf16[2,16,2,32,1024]{4,3,2,1,0:T(8,128)(2,1)S(1)}, bf16[2,16,2,32,1024]{4,3,2,1,0:T(8,128)(2,1)}, u32[]{:S(2)}) %copy-start) | copy-done | bytes 4194328
  203.2 5.0 %shard_map.92 = bf16[2,32,32,1024]{3,2,1,0:T(8,128)(2,1)} custom-call(bf16[256,256]{1,0:T(8,128)(2,1)S(1)} %copy-done.3, bf16[2,16,2,32,1024]{4,3,2,1,0:T(8,128)(2,1)S(1)} %copy-done), custom_call_target="tpu_custom_call" | custom-call | tf_op jit(solution)/shard_map/pallas_call | solution.py:328
Async XLA Ops:
  0.0 1.6 copy-start.1
  1.6 0.9 copy-start.2
  2.5 0.9 copy-start.4
  3.4 0.8 copy-start.5
  4.2 0.8 copy-start.6
  5.1 0.7 copy-start.7
  5.7 0.7 copy-start.8
  6.4 194.6 %copy-start.3 = (bf16[256,256]{1,0:T(8,128)(2,1)S(1)}, bf16[256,256]{1,0:T(8,128)(2,1)}, u32[]{:S(2)}) copy-start(bf16[256,256]{1,0:T(8,128)(2,1)} %constant.15.restore) | copy-start | bytes 393220
  201.0 2.2 %copy-start = (bf16[2,16,2,32,1024]{4,3,2,1,0:T(8,128)(2,1)S(1)}, bf16[2,16,2,32,1024]{4,3,2,1,0:T(8,128)(2,1)}, u32[]{:S(2)}) copy-start(bf16[2,16,2,32,1024]{4,3,2,1,0:T(8,128)(2,1)} %shard_map.91.block) | copy-start | bytes 12582916

commit v2 on v1

--- a/solution.py
+++ b/solution.py
@@ -48,14 +48,22 @@
     for target in lane[q == 7]:
         source = target + 57
         faces_y[source if source < CHUNK else CHUNK + source, target] = 1.0
-    return as_table(slopes), as_table(faces_x), as_table(faces_y)
+    return slopes, faces_x, faces_y
 
 
 def swap_table():
     row = np.arange(GROUP * GROUP)
     table = np.zeros((GROUP * GROUP, GROUP * GROUP))
     table[row, row % GROUP * GROUP + row // GROUP] = 1.0
-    return as_table(table)
+    return table
+
+
+def joined_tables():
+    slopes, faces_x, faces_y = lane_tables()
+    faces = np.zeros((3 * CHUNK, TILE))
+    faces[:, :CHUNK] = faces_y
+    faces[: 2 * CHUNK, CHUNK:] = faces_x
+    return as_table(np.concatenate([swap_table(), slopes, faces], axis=0))
 
 
 def restore_table(each):
@@ -69,10 +77,10 @@
 
 def sweep_kernel(
     n, strips, each,
-    fields, vel_x, vel_y, collision, slopes, faces_x, faces_y, swap,
+    fields_in, vel_x_in, vel_y_in, collision_in, tables_in,
     result,
-    columns, packed, gathered, mixed, coefs,
-    edge_send, edge_recv, out_send, out_recv, back_send, back_recv, own_sem,
+    fields, vel_x, vel_y, collision, tables, columns, packed, gathered, mixed, coefs,
+    edge_send, edge_recv, out_send, out_recv, back_send, back_recv, own_sem, load_sem,
 ):
     me = lax.axis_index("wide")
     strip = lax.axis_index("narrow")
@@ -80,7 +88,36 @@
     rows = pairs * local
     speeds = n * local
     chunks = lanes // CHUNK
+    groups = local // GROUP
+    swap = tables.at[pl.ds(0, TILE), :]
+    slopes = tables.at[pl.ds(TILE, CHUNK), :]
+    faces_y = tables.at[pl.ds(TILE + CHUNK, 3 * CHUNK), pl.ds(0, CHUNK)]
+    faces_x = tables.at[pl.ds(TILE + CHUNK, 2 * CHUNK), pl.ds(CHUNK, CHUNK)]
+    loads = [pltpu.make_async_copy(tables_in, tables, load_sem.at[0])]
+    for s in range(pairs):
+        for g in range(groups):
+            part = (s, pl.ds(g * GROUP, GROUP))
+            loads.append(
+                pltpu.make_async_copy(
+                    fields_in.at[part], fields.at[part], load_sem.at[1 + s * groups + g]
+                )
+            )
+    for k, (source, target) in enumerate(
+        ((vel_x_in, vel_x), (vel_y_in, vel_y), (collision_in, collision))
+    ):
+        loads.append(
+            pltpu.make_async_copy(source, target, load_sem.at[1 + pairs * groups + k])
+        )
+    for load in loads:
+        load.start()
     above, below = lax.rem(strip + 1, strips), lax.rem(strip + strips - 1, strips)
+
+    half = n // 2
+    upper, place = me // half, lax.rem(me, half)
+
+    def partner(i):
+        near = i // half
+        return lax.rem(upper + 1 - near, 2) * half + lax.rem(place + i + near, half)
 
     barrier = pltpu.get_barrier_semaphore()
 
@@ -94,8 +131,11 @@
     for neighbour in (above, below):
         pl.semaphore_signal(barrier, inc=1, device_id={"narrow": neighbour}, device_id_type=MESH)
 
+    loads[0].wait()
     for s in range(pairs):
-        for g in range(local // GROUP):
+        for g in range(groups):
+            loads[1 + s * groups + g].wait()
+
             def turn(h, carry):
                 at = pl.multiple_of(h * GROUP, GROUP)
                 for t in range(lanes // TILE):
@@ -124,6 +164,8 @@
         column = jnp.sum(jnp.where(eye, spread, 0.0), axis=1, keepdims=True)
         return jnp.broadcast_to(jnp.concatenate([column, -column], axis=0), (rows, CHUNK))
 
+    loads[-3].wait()
+    loads[-2].wait()
     lift = time_step * lift_gain
     own = jnp.ones((rows, CHUNK), jnp.float32)
     for k, (speed, node) in enumerate(((signed(vel_x), node_p), (signed(vel_y), node_q))):
@@ -167,7 +209,7 @@
 
     for c in range(each):
         def transport(i, carry):
-            d = lax.rem(me + i, n)
+            d = partner(i)
             if c == 0:
                 @pl.when(d == 0)
                 def _():
@@ -201,13 +243,13 @@
                     pairs, local, CHUNK
                 )
 
-            @pl.when(i < n)
+            @pl.when(i < n - 1)
             def _():
                 outward(c, d, me).start()
 
             return carry
 
-        lax.fori_loop(1, n + 1, transport, 0)
+        lax.fori_loop(0, n, transport, 0)
         pltpu.make_async_copy(
             packed.at[c, me],
             gathered.at[c, :, pl.ds(pl.multiple_of(me * local, GROUP), local), :],
@@ -221,6 +263,7 @@
             device_id={"wide": d}, device_id_type=MESH,
         )
 
+    loads[-1].wait()
     for c in range(each):
         pltpu.make_async_copy(
             packed.at[c, me],
@@ -236,7 +279,7 @@
         lax.fori_loop(1, n, arrive, 0)
 
         def collide(i, carry):
-            d = lax.rem(me + i, n)
+            d = partner(i)
             left = jnp.concatenate(
                 [
                     collision[pl.ds(pl.multiple_of(s * speeds + d * local, GROUP), local), :]
@@ -252,13 +295,13 @@
                 )
                 mixed[c, d, :, :, part] = total.astype(jnp.bfloat16).reshape(pairs, local, TILE)
 
-            @pl.when(i < n)
+            @pl.when(i < n - 1)
             def _():
                 back(c, d, me).start()
 
             return carry
 
-        lax.fori_loop(1, n + 1, collide, 0)
+        lax.fori_loop(0, n, collide, 0)
         pltpu.make_async_copy(
             mixed.at[c, me], result.at[c, me], own_sem.at[each + c]
         ).start()
@@ -296,14 +339,19 @@
     each = width // n
     rows = pairs * local
     bf16 = jnp.bfloat16
-    vmem = pl.BlockSpec(memory_space=pltpu.VMEM)
+    hbm = pl.BlockSpec(memory_space=pltpu.HBM)
     dma = pltpu.SemaphoreType.DMA
     returned = pl.pallas_call(
         functools.partial(sweep_kernel, n, strips, each),
         out_shape=jax.ShapeDtypeStruct((each, n, pairs, local, lanes), bf16),
-        in_specs=[vmem] * 8,
-        out_specs=pl.BlockSpec(memory_space=pl.ANY),
+        in_specs=[hbm] * 5,
+        out_specs=hbm,
         scratch_shapes=[
+            pltpu.VMEM(fields.shape, bf16),
+            pltpu.VMEM((1, local), jnp.float32),
+            pltpu.VMEM((1, local), jnp.float32),
+            pltpu.VMEM(collision.shape, bf16),
+            pltpu.VMEM((2 * TILE + 2 * CHUNK, TILE), bf16),
             pltpu.VMEM((width + 2, rows, lanes), bf16),
             pltpu.VMEM((each, n, pairs, local, lanes), bf16),
             pltpu.VMEM((each, pairs, n * local, lanes), bf16),
@@ -316,13 +364,14 @@
             dma((each, n)),
             dma((each, n)),
             dma((2 * each,)),
+            dma((4 + pairs * (local // GROUP),)),
         ],
         compiler_params=pltpu.CompilerParams(
-            collective_id=0, has_side_effects=True, vmem_limit_bytes=48 * 1024 * 1024
+            collective_id=0, has_side_effects=True, vmem_limit_bytes=62 * 1024 * 1024
         ),
     )(
         fields, vel_x.reshape(1, local), vel_y.reshape(1, local), collision,
-        *lane_tables(), swap_table(),
+        joined_tables(),
     )
     owners = GROUP // each
     return pl.pallas_call(
@@ -334,7 +383,7 @@
             pl.BlockSpec((each, owners, 1, GROUP, lanes), lambda s, g, h: (0, h, s, g, 0)),
         ],
         out_specs=pl.BlockSpec((1, GROUP, GROUP, lanes), lambda s, g, h: (s, g, h, 0)),
-        compiler_params=pltpu.CompilerParams(vmem_limit_bytes=16 * 1024 * 1024),
+        compiler_params=pltpu.CompilerParams(vmem_limit_bytes=60 * 1024 * 1024),
     )(restore_table(each), returned)
 
 

time: 209 us -> 203 us (0.971)
  the two profiles are of different devices: /device:TPU:11 before, /device:TPU:1 now
where the time goes in v2:
time: 203 us
  Pallas kernels  203 us (100%)
    pallas_call x1, Pallas kernels, shards(): pl.pallas_call(functools.partial(sweep_kernel, n, strips, each), out_shap...  195 us
    pallas_call x1, Pallas kernels, shards(): pl.pallas_call(restore_kernel, grid=(pairs, local // GROUP, width // GROU...  7.55 us

profile of v2, /device:TPU:1, one launch (start us, length us, event | category | flops | bytes accessed | tf_op | source)
XLA Modules:
  0.0 203.0 jit_solution(7738974121064465966)
XLA Ops:
  0.0 195.4 %shard_map.64.block = bf16[2,16,2,32,1024]{4,3,2,1,0:T(8,128)(2,1)} custom-call(bf16[2,32,32,1024]{3,2,1,0:T(8,128)(2,1)} %fields_in.1, f32[1,32]{1,0:T(1,128)} %bitcast.2, f32[1,32]{1,0:T(1,128)} %bitcast.3, bf16[1024,1024]{1,0:T(8,128)(2,1)} %collision_in.1, bf16[768,256]{1,0:T(8,128)(2,1)} %constant.7.tables_in), custom_call_target="tpu_custom_call" | custom-call | tf_op jit(solution)/shard_map/pallas_call | solution.py:344
  195.5 7.6 %shard_map.65 = bf16[2,32,32,1024]{3,2,1,0:T(8,128)(2,1)} custom-call(bf16[256,256]{1,0:T(8,128)(2,1)} %constant.6.restore, bf16[2,16,2,32,1024]{4,3,2,1,0:T(8,128)(2,1)} %shard_map.64.block), custom_call_target="tpu_custom_call" | custom-call | tf_op jit(solution)/shard_map/pallas_call | solution.py:377

commit v3 on v2

--- a/solution.py
+++ b/solution.py
@@ -323,13 +323,46 @@
         lax.fori_loop(1, n, finish, 0)
 
 
-def restore_kernel(restore, block, out):
-    rows = GROUP * GROUP
-    lanes = out.shape[-1]
-    turned = jnp.dot(
-        restore[...], block[...].reshape(rows, lanes), preferred_element_type=jnp.float32
-    )
-    out[...] = turned.astype(jnp.bfloat16).reshape(out.shape)
+def restore_kernel(table_in, returned, result, table, held, turned, table_sem, in_sem, out_sem):
+    each, n, pairs, local, lanes = held.shape
+    owners = GROUP // each
+    blocks = [
+        (s, g, h)
+        for s in range(pairs)
+        for g in range(local // GROUP)
+        for h in range(n // owners)
+    ]
+
+    def fetch(k):
+        s, g, h = blocks[k]
+        part = (slice(None), pl.ds(h * owners, owners), s, pl.ds(g * GROUP, GROUP))
+        return pltpu.make_async_copy(returned.at[part], held.at[part], in_sem.at[k])
+
+    def place(k):
+        s, g, h = blocks[k]
+        part = (s, pl.ds(g * GROUP, GROUP), pl.ds(h * GROUP, GROUP))
+        return pltpu.make_async_copy(turned.at[part], result.at[part], out_sem.at[k])
+
+    load = pltpu.make_async_copy(table_in, table, table_sem)
+    load.start()
+    for k in range(len(blocks)):
+        fetch(k).start()
+    load.wait()
+    for k, (s, g, h) in enumerate(blocks):
+        fetch(k).wait()
+        for t in range(lanes // TILE):
+            part = pl.ds(t * TILE, TILE)
+            block = held[:, pl.ds(h * owners, owners), s, pl.ds(g * GROUP, GROUP), part]
+            rows = jnp.dot(
+                table[...], block.reshape(GROUP * GROUP, TILE),
+                preferred_element_type=jnp.float32,
+            )
+            turned[s, pl.ds(g * GROUP, GROUP), pl.ds(h * GROUP, GROUP), part] = rows.astype(
+                jnp.bfloat16
+            ).reshape(GROUP, GROUP, TILE)
+        place(k).start()
+    for k in range(len(blocks)):
+        place(k).wait()
 
 
 def shards(fields, vel_x, vel_y, collision):
@@ -373,16 +406,20 @@
         fields, vel_x.reshape(1, local), vel_y.reshape(1, local), collision,
         joined_tables(),
     )
-    owners = GROUP // each
+    blocks = pairs * (local // GROUP) * (width // GROUP)
     return pl.pallas_call(
         restore_kernel,
-        grid=(pairs, local // GROUP, width // GROUP),
         out_shape=jax.ShapeDtypeStruct(fields.shape, bf16),
-        in_specs=[
-            pl.BlockSpec((GROUP * GROUP, GROUP * GROUP), lambda s, g, h: (0, 0)),
-            pl.BlockSpec((each, owners, 1, GROUP, lanes), lambda s, g, h: (0, h, s, g, 0)),
+        in_specs=[hbm] * 2,
+        out_specs=hbm,
+        scratch_shapes=[
+            pltpu.VMEM((GROUP * GROUP, GROUP * GROUP), bf16),
+            pltpu.VMEM((each, n, pairs, local, lanes), bf16),
+            pltpu.VMEM(fields.shape, bf16),
+            dma,
+            dma((blocks,)),
+            dma((blocks,)),
         ],
-        out_specs=pl.BlockSpec((1, GROUP, GROUP, lanes), lambda s, g, h: (s, g, h, 0)),
         compiler_params=pltpu.CompilerParams(vmem_limit_bytes=60 * 1024 * 1024),
     )(restore_table(each), returned)
 

time: 203 us -> 200 us (0.985)
  Pallas kernels: 203 us -> 200 us
    pallas_call x1, Pallas kernels: 7.55 us -> 4.51 us  [shards(): pl.pallas_call(restore_kernel, out_shape=jax.ShapeDtypeStruct(fields.shap...]
where the time goes in v3:
time: 200 us
  Pallas kernels  200 us (100%)
    pallas_call x1, Pallas kernels, shards(): pl.pallas_call(functools.partial(sweep_kernel, n, strips, each), out_shap...  195 us
    pallas_call x1, Pallas kernels, shards(): pl.pallas_call(restore_kernel, out_shape=jax.ShapeDtypeStruct(fields.shap...  4.51 us

profile of v3, /device:TPU:1, one launch (start us, length us, event | category | flops | bytes accessed | tf_op | source)
XLA Modules:
  0.0 200.0 jit_solution(2682694923609451177)
XLA Ops:
  0.0 195.4 %shard_map.64.returned = bf16[2,16,2,32,1024]{4,3,2,1,0:T(8,128)(2,1)} custom-call(bf16[2,32,32,1024]{3,2,1,0:T(8,128)(2,1)} %fields_in.1, f32[1,32]{1,0:T(1,128)} %bitcast.2, f32[1,32]{1,0:T(1,128)} %bitcast.3, bf16[1024,1024]{1,0:T(8,128)(2,1)} %collision_in.1, bf16[768,256]{1,0:T(8,128)(2,1)} %constant.7.tables_in), custom_call_target="tpu_custom_call" | custom-call | tf_op jit(solution)/shard_map/pallas_call | solution.py:377
  195.5 4.5 %shard_map.65 = bf16[2,32,32,1024]{3,2,1,0:T(8,128)(2,1)} custom-call(bf16[256,256]{1,0:T(8,128)(2,1)} %constant.6.table_in, bf16[2,16,2,32,1024]{4,3,2,1,0:T(8,128)(2,1)} %shard_map.64.returned), custom_call_target="tpu_custom_call" | custom-call | tf_op jit(solution)/shard_map/pallas_call | solution.py:410

commit v4 on v3

--- a/solution.py
+++ b/solution.py
@@ -108,7 +108,7 @@
         loads.append(
             pltpu.make_async_copy(source, target, load_sem.at[1 + pairs * groups + k])
         )
-    for load in loads:
+    for load in (*loads[-3:-1], *loads[:-3], loads[-1]):
         load.start()
     above, below = lax.rem(strip + 1, strips), lax.rem(strip + strips - 1, strips)
 
@@ -130,27 +130,6 @@
     lax.fori_loop(1, n, greet, 0)
     for neighbour in (above, below):
         pl.semaphore_signal(barrier, inc=1, device_id={"narrow": neighbour}, device_id_type=MESH)
-
-    loads[0].wait()
-    for s in range(pairs):
-        for g in range(groups):
-            loads[1 + s * groups + g].wait()
-
-            def turn(h, carry):
-                at = pl.multiple_of(h * GROUP, GROUP)
-                for t in range(lanes // TILE):
-                    part = pl.ds(t * TILE, TILE)
-                    block = fields[s, pl.ds(g * GROUP, GROUP), pl.ds(at, GROUP), part]
-                    turned = jnp.dot(
-                        swap[...], block.reshape(GROUP * GROUP, TILE),
-                        preferred_element_type=jnp.float32,
-                    )
-                    columns[
-                        pl.ds(at + 1, GROUP), pl.ds(s * local + g * GROUP, GROUP), part
-                    ] = turned.astype(jnp.bfloat16).reshape(GROUP, GROUP, TILE)
-                return carry
-
-            lax.fori_loop(0, width // GROUP, turn, 0)
 
     lane = lax.broadcasted_iota(jnp.int32, (rows, CHUNK), 1)
     node_p = (lane >> 3) & 7
@@ -176,6 +155,23 @@
         coefs[1 + k] = -time_step * speed
         coefs[3 + k] = face
     coefs[0] = own
+
+    loads[0].wait()
+    for s in range(pairs):
+        for g in range(groups):
+            loads[1 + s * groups + g].wait()
+            for h in range(width // GROUP):
+                at = h * GROUP
+                for t in range(lanes // TILE):
+                    part = pl.ds(t * TILE, TILE)
+                    block = fields[s, pl.ds(g * GROUP, GROUP), pl.ds(at, GROUP), part]
+                    turned = jnp.dot(
+                        swap[...], block.reshape(GROUP * GROUP, TILE),
+                        preferred_element_type=jnp.float32,
+                    )
+                    columns[
+                        pl.ds(at + 1, GROUP), pl.ds(s * local + g * GROUP, GROUP), part
+                    ] = turned.astype(jnp.bfloat16).reshape(GROUP, GROUP, TILE)
 
     pl.semaphore_wait(barrier, n + 1)
 

time: 200 us -> 198 us (0.990)
  Pallas kernels: 200 us -> 198 us
    pallas_call x1, Pallas kernels: 195 us -> 193 us  [shards(): pl.pallas_call(functools.partial(sweep_kernel, n, strips, each), out_shap...]
where the time goes in v4:
time: 198 us
  Pallas kernels  198 us (100%)
    pallas_call x1, Pallas kernels, shards(): pl.pallas_call(functools.partial(sweep_kernel, n, strips, each), out_shap...  193 us
    pallas_call x1, Pallas kernels, shards(): pl.pallas_call(restore_kernel, out_shape=jax.ShapeDtypeStruct(fields.shap...  4.51 us

profile of v4, /device:TPU:1, one launch (start us, length us, event | category | flops | bytes accessed | tf_op | source)
XLA Modules:
  0.0 197.6 jit_solution(9863470593064252155)
XLA Ops:
  0.0 193.1 %shard_map.64.returned = bf16[2,16,2,32,1024]{4,3,2,1,0:T(8,128)(2,1)} custom-call(bf16[2,32,32,1024]{3,2,1,0:T(8,128)(2,1)} %fields_in.1, f32[1,32]{1,0:T(1,128)} %bitcast.2, f32[1,32]{1,0:T(1,128)} %bitcast.3, bf16[1024,1024]{1,0:T(8,128)(2,1)} %collision_in.1, bf16[768,256]{1,0:T(8,128)(2,1)} %constant.7.tables_in), custom_call_target="tpu_custom_call" | custom-call | tf_op jit(solution)/shard_map/pallas_call | solution.py:373
  193.1 4.5 %shard_map.65 = bf16[2,32,32,1024]{3,2,1,0:T(8,128)(2,1)} custom-call(bf16[256,256]{1,0:T(8,128)(2,1)} %constant.6.table_in, bf16[2,16,2,32,1024]{4,3,2,1,0:T(8,128)(2,1)} %shard_map.64.returned), custom_call_target="tpu_custom_call" | custom-call | tf_op jit(solution)/shard_map/pallas_call | solution.py:406
